TPU v7x, 768 devices: a whole 4x8x12 slice. The times are simulated.
768 devices in a mesh: leaf: 384 (over x, z, y), grp: 2 (over core).
Axes of the slice: x: 4, y: 8, z: 12, core: 2. Of those that a mesh axis runs over, the one named last changes fastest.
Arguments:
- charges: bfloat16 [1536, 8, 256], P(('leaf', 'grp')), may hold values from -6 to 6
- leaf_basis: bfloat16 [1536, 64, 256], P(('leaf', 'grp')), may hold values from -0.375 to 0.375
- transfers: float32 [768, 3, 64, 64], P(('leaf', 'grp')), may hold values from -0.75 to 0.75
- near_blocks: bfloat16 [1536, 6, 256, 256], P(('leaf', 'grp')), may hold values from -0.15625 to 0.15625
- near_list: int32 [1536, 6], P(('leaf', 'grp')), may hold values from 0 to 1535, as said below
- near_count: int32 [1536], P(('leaf', 'grp')), may hold values from 1 to 6, as said below
- dev_coupling: float32 [768, 8, 64, 64], P(('leaf', 'grp')), may hold values from -0.25 to 0.25
- dev_list: int32 [768, 8], P(('leaf', 'grp')), may hold values from 0 to 767, as said below
- dev_count: int32 [768], P(('leaf', 'grp')), may hold values from 1 to 8, as said below
- pair_coupling: float32 [384, 16, 64, 64], P('leaf', 'grp'), may hold values from -0.1875 to 0.1875
- pair_list: int32 [384, 16], P('leaf', 'grp'), may hold values from 0 to 383, as said below
- pair_count: int32 [384], P('leaf'), may hold values from 1 to 16, as said below
Outputs:
- potentials: float32 [1536, 8, 256], P(('leaf', 'grp'))
Inputs may be any that keep to these rules, and one draw needn't show every extreme that they name: `near_list`: row i names leaves at most 2 places from i; slot 0 is i itself. `near_count`: slots from the count on are unused; some leaf uses all of them. `dev_list`: names subtrees 1 to 5 places from the subtree itself or 768 // 2 places on, counted cyclically; some row names a subtree 5 places on, some row one 5 places back, and some row one half the subtrees on. `dev_count`: slots from the count on are unused; some subtree uses all of them. `pair_list`: names pairs 1 to 5 places from the pair itself or 384 // 2 places on, counted cyclically; some row names a pair 5 places on, some row one 5 places back, and some row one half the pairs on. `pair_count`: slots from the count on are unused; some pair uses all of them.
All inputs are finite; a program needn't handle non-finite values.
Results may differ from a plain program's by a relative error of at most 0.0004.
Values may be sent and summed in bfloat16 or wider, within the bound.
A program may use at most 32 MiB of HBM per device.

v0:
```python
import jax
import jax.numpy as jnp
from jax import lax
from jax.sharding import PartitionSpec as P

exact_mode = lax.Precision.HIGHEST


def from_partner(value, axis, apart):
    return lax.ppermute(value, axis, [(i, i ^ 1 << apart) for i in range(lax.axis_size(axis))])


def extended_2(value, sides, width):
    for axis, dim in sides:
        size, length = (lax.axis_size(axis), value.shape[dim])
        up = [(i, (i + 1) % size) for i in range(size - 1)]
        down = [(j, i) for i, j in up]
        last = lax.slice_in_dim(value, length - width, length, axis=dim)
        first = lax.slice_in_dim(value, 0, width, axis=dim)
        before = lax.ppermute(last, axis, up)
        after = lax.ppermute(first, axis, down)
        value = jnp.concatenate([before, value, after], axis=dim)
    return value


def per_device(
    charges,
    leaf_basis,
    transfers,
    near_blocks,
    near_list,
    near_count,
    dev_coupling,
    dev_list,
    dev_count,
    pair_coupling,
    pair_list,
    pair_count,
):
    leaf_rows, vectors, panels = charges.shape
    ranks = leaf_basis.shape[1]
    far_slots = dev_list.shape[1]
    near_slots = near_list.shape[1]
    device = lax.axis_index(("leaf", "grp"))
    core_index = lax.axis_index("grp")
    transfer_set = transfers[0]
    basis_float = leaf_basis.astype(jnp.float32)
    leaf_coeff = jnp.einsum("lrp,lkp->lrk", charges, leaf_basis, preferred_element_type=jnp.float32)
    section_coeff = leaf_coeff
    offset = 0
    members = leaf_rows
    sections = []
    while members > 1:
        matrices = transfer_set[offset : offset + members]
        lifted_section = jnp.einsum("nrk,nkj->nrj", section_coeff, matrices, precision=exact_mode)
        section_coeff = lifted_section.reshape(members // 2, 2, vectors, ranks).sum(axis=1)
        sections.append((offset, members))
        offset = offset + members
        members = members // 2
    last_transfer = transfer_set[offset]
    lifted = jnp.einsum("nrk,kj->nrj", section_coeff, last_transfer, precision=exact_mode)
    dev_targets = dev_list[0]
    pair_targets = pair_list[0]
    dev_piece = lax.all_gather(section_coeff, ("leaf", "grp"), axis=0, tiled=True)
    lift_piece = lax.all_gather(lifted, ("leaf", "grp"), axis=0, tiled=True)
    source_ids = jnp.arange(dev_piece.shape[0], dtype=jnp.int32)
    pick_dev = (dev_targets[:, None] == source_ids[None, :]).astype(jnp.float32)
    pick_pair = (pair_targets[:, None] == source_ids[None, :] // 2).astype(jnp.float32)
    dev_sources = jnp.einsum("sn,nrk->srk", pick_dev, dev_piece, precision=exact_mode)
    pair_sources = jnp.einsum("sn,nrk->srk", pick_pair, lift_piece, precision=exact_mode)
    slot_index = jnp.arange(far_slots, dtype=jnp.int32)
    dev_mask = (slot_index < dev_count[0]).astype(jnp.float32)
    dev_field = jnp.einsum(
        "srk,skj->rj", dev_sources * dev_mask[:, None, None], dev_coupling[0], precision=exact_mode
    )
    pair_mask = (core_index * far_slots + slot_index < pair_count[0]).astype(jnp.float32)
    partial_value = jnp.einsum(
        "srk,skj->rj",
        pair_sources * pair_mask[:, None, None],
        pair_coupling[0],
        precision=exact_mode,
    )
    pair_field = partial_value + from_partner(partial_value, "grp", 0)
    root_field = dev_field + jnp.einsum(
        "rj,kj->rk", pair_field, last_transfer, precision=exact_mode
    )
    section_field = root_field[None]
    for offset, members in reversed(sections):
        spread = jnp.repeat(section_field, 2, axis=0)
        section_field = jnp.einsum(
            "nrj,nkj->nrk", spread, transfer_set[offset : offset + members], precision=exact_mode
        )
    far_part = jnp.einsum("lrk,lkp->lrp", section_field, basis_float, precision=exact_mode)
    extended = extended_2(charges, ((("leaf", "grp"), 0),), leaf_rows)
    local_index = near_list - (device * leaf_rows - leaf_rows)
    picked = extended[local_index]
    used = jnp.arange(near_slots, dtype=jnp.int32)[None, :] < near_count[:, None]
    picked = jnp.where(used[:, :, None, None], picked, jnp.zeros_like(picked))
    near_part = jnp.einsum(
        "lsrp,lspq->lrq", picked, near_blocks, preferred_element_type=jnp.float32
    )
    return near_part + far_part


def solution(mesh):
    return jax.shard_map(
        per_device,
        mesh=mesh,
        in_specs=(
            P(("leaf", "grp"), None, None),
            P(("leaf", "grp"), None, None),
            P(("leaf", "grp"), None, None, None),
            P(("leaf", "grp"), None, None, None),
            P(("leaf", "grp"), None),
            P(("leaf", "grp")),
            P(("leaf", "grp"), None, None, None),
            P(("leaf", "grp"), None),
            P(("leaf", "grp")),
            P("leaf", "grp", None, None),
            P("leaf", "grp"),
            P("leaf"),
        ),
        out_specs=P(("leaf", "grp"), None, None),
        check_vma=False,
    )
```

profile of v0, /device:TPU:1, one launch (start us, length us, event | category | flops | bytes accessed | tf_op | source)
XLA Modules:
  0.0 368.2 jit_solution(3292614878735540467)
XLA Ops:
  6.5 1.1 fusion.35
  7.7 1.1 convolution_bitcast_fusion.3
  8.7 1.5 fusion.15
  10.2 0.0 all-gather.7.cloned.1.call-update
  10.3 0.0 all-gather.5.cloned.1.call-start
  10.3 0.7 all-gather.5.cloned.1.call-update
  11.0 12.4 %collective-permute-start.1 = (bf16[2,8,256]{2,1,0:T(8,128)(2,1)}, bf16[2,8,256]{2,1,0:T(8,128)(2,1)S(1)}, u32[]{:S(2)}, u32[]{:S(2)}) collective-permute-start(bf16[2,8,256]{2,1,0:T(8,128)(2,1)} %param.12), channel_id=1, source_target_pairs={{1,0},{2,1},{3,2},{4,3},{5,4},{6,5},{7,6},{8,7},{9,8},{10,9},{11,1... | collective-permute-start | bytes 24584 | tf_op jit(solution)/shard_map/ppermute | solution.py:21
  23.4 1.9 collective-permute-start
  26.7 0.7 compare_select_fusion
  27.4 0.1 reshape.85
  27.5 0.7 iota_compare_fusion.1
  28.2 0.7 pad_maximum_fusion
  28.9 0.6 gather_fusion
  29.5 157.7 %all-gather.7.cloned.1.call-done = f32[6144,64]{1,0:T(8,128)} async-done(((f32[8,64]{1,0:T(8,128)}), f32[6144,64]{1,0:T(8,128)}) %all-gather.7.cloned.1.call-update) | async-done | bytes 1572880 | tf_op jit(solution)/shard_map/all_gather | solution.py:65
  187.2 3.3 fusion
  190.5 0.3 convolution_bitcast_fusion.1
  190.8 2.1 collective-permute-start.2
  192.9 163.3 %all-gather.5.cloned.1.call-done = f32[6144,64]{1,0:T(8,128)} async-done(((f32[8,64]{1,0:T(8,128)}), f32[6144,64]{1,0:T(8,128)}) %all-gather.5.cloned.1.call-update) | async-done | bytes 1572880 | tf_op jit(solution)/shard_map/all_gather | solution.py:64
  356.2 3.3 fusion.2
  359.5 0.3 convolution_bitcast_fusion.2
  359.8 0.1 convolution_add_fusion
  360.0 0.2 fusion.7
  360.2 0.2 fusion.36
  360.4 1.0 fusion.4
  (22 shorter events, 0.1 us)
Async XLA Ops:
  6.5 353.8 %copy-start = (bf16[2,6,256,256]{3,2,1,0:T(8,128)(2,1)S(1)}, bf16[2,6,256,256]{3,2,1,0:T(8,128)(2,1)}, u32[]{:S(2)}) copy-start(bf16[2,6,256,256]{3,2,1,0:T(8,128)(2,1)} %param.15) | copy-start | bytes 4718596
  6.5 183.9 %copy-start.2 = (f32[1,8,64,64]{3,2,1,0:T(8,128)S(1)}, f32[1,8,64,64]{3,2,1,0:T(8,128)}, u32[]{:S(2)}) copy-start(f32[1,8,64,64]{3,2,1,0:T(8,128)} %param.21) | copy-start | bytes 393220
  6.5 349.7 %copy-start.6 = (s32[1,8]{1,0:T(1,128)S(1)}, s32[1,8]{1,0:T(1,128)}, u32[]{:S(2)}) copy-start(s32[1,8]{1,0:T(1,128)} %param.19) | copy-start | bytes 100
  6.5 180.6 %all-gather.7.cloned.1.call-start = ((), (), s32[]{:S(2)}) async-start(), calls=%async_computation.1 | async-start | bytes 3149824 | tf_op jit(solution)/shard_map/all_gather | solution.py:65
  8.7 1.6 copy-start.5
  10.3 346.0 %all-gather.5.cloned.1.call-start = ((), (), s32[]{:S(2)}) async-start(), calls=%async_computation | async-start | bytes 3149824 | tf_op jit(solution)/shard_map/all_gather | solution.py:64
  11.0 17.2 %collective-permute-start.1 = (bf16[2,8,256]{2,1,0:T(8,128)(2,1)}, bf16[2,8,256]{2,1,0:T(8,128)(2,1)S(1)}, u32[]{:S(2)}, u32[]{:S(2)}) collective-permute-start(bf16[2,8,256]{2,1,0:T(8,128)(2,1)} %param.12), channel_id=1, source_target_pairs={{1,0},{2,1},{3,2},{4,3},{5,4},{6,5},{7,6},{8,7},{9,8},{10,9},{11,1... | collective-permute-start | bytes 24584 | tf_op jit(solution)/shard_map/ppermute | solution.py:21
  23.4 4.8 %collective-permute-start = (bf16[2,8,256]{2,1,0:T(8,128)(2,1)}, bf16[2,8,256]{2,1,0:T(8,128)(2,1)S(1)}, u32[]{:S(2)}, u32[]{:S(2)}) collective-permute-start(bf16[2,8,256]{2,1,0:T(8,128)(2,1)} %param.12), channel_id=1, source_target_pairs={{0,1},{1,2},{2,3},{3,4},{4,5},{5,6},{6,7},{7,8},{8,9},{9,10},{10,1... | collective-permute-start | bytes 24584 | tf_op jit(solution)/shard_map/ppermute | solution.py:20
  187.2 172.3 %copy-start.3 = (f32[1,8,64,64]{3,2,1,0:T(8,128)S(1)}, f32[1,8,64,64]{3,2,1,0:T(8,128)}, u32[]{:S(2)}) copy-start(f32[1,8,64,64]{3,2,1,0:T(8,128)} %param.18) | copy-start | bytes 393220
  187.2 172.7 %copy-start.1 = (f32[1,3,64,64]{3,2,1,0:T(8,128)S(1)}, f32[1,3,64,64]{3,2,1,0:T(8,128)}, u32[]{:S(2)}) copy-start(f32[1,3,64,64]{3,2,1,0:T(8,128)} %param.14) | copy-start | bytes 147460
  187.2 173.0 %copy-start.4 = (bf16[2,64,256]{2,1,0:T(8,128)(2,1)S(1)}, bf16[2,64,256]{2,1,0:T(8,128)(2,1)}, u32[]{:S(2)}) copy-start(bf16[2,64,256]{2,1,0:T(8,128)(2,1)} %param.13) | copy-start | bytes 196612
  190.8 169.0 %collective-permute-start.2 = (f32[8,64]{1,0:T(8,128)S(1)}, f32[8,64]{1,0:T(8,128)S(1)}, u32[]{:S(2)}, u32[]{:S(2)}) collective-permute-start(f32[8,64]{1,0:T(8,128)S(1)} %convolution_bitcast_fusion.1), channel_id=1, source_target_pairs={{0,1},{1,0},{2,3},{3,2},{4,5},{5,4},{6,7},{7,6},{8,9},{9,8},{10,11... | collective-permute-start | bytes 6152 | tf_op jit(solution)/shard_map/ppermute | solution.py:10
Sparse Core Ops, SparseCore 0:
  12.9 174.1 all-gather.6
  192.7 163.4 all-gather.4
where the time goes:
time: 369 us; the launch traced here: 368 us
  waiting for transfers between devices  322 us (87%)
  starting transfers between devices  16.5 us (4%)
  between operations  14.8 us (4%)
  matrix products  12.4 us (3%)
    all_gather x1, waiting for transfers between devices, per_device(): lax.all_gather(section_coeff, ('leaf', 'grp'), axis=0, tiled=True)  163 us
    all_gather x1, waiting for transfers between devices, per_device(): lift_piece = lax.all_gather(lifted, ('leaf', 'grp'), axis=0, tiled=True)  158 us
    ppermute x1, starting transfers between devices, extended_2(): after = lax.ppermute(first, axis, down)  12.4 us
  transfers between devices with their start and end apart: 5, of which 2 were waited for; matrix products, arithmetic and copies ran while one was open for 3% of the time, Pallas kernels for 0%

commit v1 on v0

v1 whole, which is shorter than its diff:
```python
import functools

import jax
import jax.numpy as jnp
from jax import lax
from jax.experimental import pallas as pl
from jax.experimental.pallas import tpu as pltpu
from jax.sharding import PartitionSpec as P

MESH = pl.DeviceIdType.MESH
REACH = 5
F32 = jnp.float32
BF16 = jnp.bfloat16
NN = (((1,), (0,)), ((), ()))
NT = (((1,), (1,)), ((), ()))
TN = (((0,), (0,)), ((), ()))


def dot(a, b, dims=NN):
    return lax.dot_general(a, b, dims, preferred_element_type=F32)


def halves(a):
    high = a.astype(BF16)
    return high, (a - high.astype(F32)).astype(BF16)


def dot3(a, b, dims=NN):
    ah, al = halves(a)
    bh, bl = halves(b)
    return dot(ah, bh, dims) + dot(al, bh, dims) + dot(ah, bl, dims)


def stacked(a):
    high = a.astype(BF16).astype(F32)
    return jnp.concatenate([high, a - high], axis=0).astype(BF16)


def folded(a):
    return a[0:8] + a[8:16]


def kernel(
    pairs,
    charges,
    basis,
    transfers,
    near_blocks,
    near_list,
    near_count,
    dev_coupling,
    dev_list,
    dev_count,
    pair_coupling,
    pair_list,
    pair_count,
    out,
    charge_buf,
    basis_buf,
    transfer_buf,
    block_buf,
    dev_buf,
    pair_buf,
    tiles,
    w_high,
    w_low,
    s_near_list,
    s_near_count,
    s_dev_list,
    s_dev_count,
    s_pair_list,
    s_pair_count,
    partner_list,
    in_sem,
    tile_send,
    tile_recv,
    charge_send,
    charge_recv,
    coupling_send,
    coupling_recv,
    list_send,
    list_recv,
):
    q = lax.axis_index("leaf")
    g = lax.axis_index("grp")
    other = 1 - g
    half = pairs // 2
    own = REACH
    last = 2 * REACH + 1

    peers = [((q, other), 2 * own + g)]
    for shift in (half, 5, -5, 4, -4, 3, -3, 2, -2, 1, -1):
        there = lax.rem(q + (shift + pairs), pairs)
        place = last if shift == half else own - shift
        for core in (g, other):
            peers.append(((there, core), 2 * place + g))
    count = len(peers)

    local = [
        (charges, charge_buf.at[1]),
        (basis, basis_buf),
        (transfers, transfer_buf),
        (pair_coupling, pair_buf.at[0]),
        (dev_coupling, dev_buf),
        (near_blocks.at[0], block_buf.at[0]),
        (near_blocks.at[1], block_buf.at[1]),
        (near_list, s_near_list),
        (near_count, s_near_count),
        (dev_list, s_dev_list),
        (dev_count, s_dev_count),
        (pair_list, s_pair_list),
        (pair_count, s_pair_count),
    ]
    local = [pltpu.make_async_copy(a, b, in_sem.at[i]) for i, (a, b) in enumerate(local)]
    for copy in local[:3]:
        copy.start()
    barrier = pltpu.get_barrier_semaphore()
    for device, _ in peers:
        pl.semaphore_signal(barrier, inc=1, device_id=device, device_id_type=MESH)
    for copy in local[3:]:
        copy.start()

    for copy in local[:3]:
        copy.wait()
    e = transfer_buf[0]
    e01 = e[0:2].reshape(128, 64)
    up = jnp.concatenate([e01, dot3(e01, e[2])], axis=1)
    own_charges = charge_buf[1].astype(F32).reshape(16, 256).astype(BF16)
    cross = dot(own_charges, basis_buf[...].reshape(128, 256), NT)
    lane = lax.broadcasted_iota(jnp.int32, (8, 128), 1)
    leaf_coeff = stacked(jnp.where(lane < 64, cross[0:8], cross[8:16]))
    up_high, up_low = halves(up)
    my_tile = 2 * own + g
    tiles[my_tile] = folded(dot(leaf_coeff, up_high) + dot(leaf_coeff, up_low))

    pl.semaphore_wait(barrier, count)
    sends = []
    for device, place in peers:
        sends.append(
            pltpu.make_async_remote_copy(
                src_ref=tiles.at[my_tile],
                dst_ref=tiles.at[place],
                send_sem=tile_send,
                recv_sem=tile_recv,
                device_id=device,
                device_id_type=MESH,
            )
        )
    step = 2 * g - 1
    beside = (lax.rem(q + step + pairs, pairs), other)
    to_partner = pltpu.make_async_remote_copy(
        src_ref=charges,
        dst_ref=charge_buf.at[2 * g],
        send_sem=charge_send.at[0],
        recv_sem=charge_recv.at[0],
        device_id=(q, other),
        device_id_type=MESH,
    )
    to_beside = pltpu.make_async_remote_copy(
        src_ref=charges,
        dst_ref=charge_buf.at[2 - 2 * g],
        send_sem=charge_send.at[1],
        recv_sem=charge_recv.at[1],
        device_id=beside,
        device_id_type=MESH,
    )
    give_list = pltpu.make_async_remote_copy(
        src_ref=pair_list,
        dst_ref=partner_list,
        send_sem=list_send,
        recv_sem=list_recv,
        device_id=(q, other),
        device_id_type=MESH,
    )
    give_coupling = pltpu.make_async_remote_copy(
        src_ref=pair_coupling,
        dst_ref=pair_buf.at[1],
        send_sem=coupling_send,
        recv_sem=coupling_recv,
        device_id=(q, other),
        device_id_type=MESH,
    )
    others = [to_beside, to_partner, give_coupling, give_list]
    for copy in sends + others:
        copy.start()

    for copy in local[3:5]:
        copy.wait()
    for copy in local[7:]:
        copy.wait()
    e2h, e2l = halves(e[2])

    def through_pair(blocks):
        rows = blocks.reshape(512, 64)
        rh, rl = halves(rows)
        return (dot(rh, e2h, NT) + dot(rl, e2h, NT) + dot(rh, e2l, NT)).reshape(8, 64, 64)

    def used(slot, total):
        return jnp.where(slot < total, 1.0, 0.0).astype(F32)

    dev_total = s_dev_count[0]
    pair_total = s_pair_count[0]
    lifted = through_pair(pair_buf[0, 0])
    for s in range(8):
        w = jnp.concatenate(
            [dev_buf[0, s] * used(s, dev_total), lifted[s] * used(8 * g + s, pair_total)], axis=0
        )
        w_high[s], w_low[s] = halves(w)

    down = [
        dot(e_part, basis_buf[l], TN)
        for l in range(2)
        for e_part in halves(e[l])
    ]
    down = jnp.concatenate([down[0] + down[1], down[2] + down[3]], axis=1)
    down_high, down_low = halves(down)

    for copy in (to_beside, to_partner):
        copy.wait_recv()
    for copy in local[5:7]:
        copy.wait()
    first = 2 * (2 * q + g) - 2
    near = []
    for l in range(2):
        total = jnp.zeros((8, 256), F32)
        for s in range(6):
            at = jnp.clip(s_near_list[l, s] - first, 0, 5)
            picked = charge_buf[at // 2, at % 2].astype(F32) * used(s, s_near_count[l])
            total += dot(picked.astype(BF16), block_buf[l, s])
        near.append(total)

    give_coupling.wait_recv()
    give_list.wait_recv()
    lifted = through_pair(pair_buf[1, 0])
    for t in range(4):
        w = jnp.concatenate(
            [lifted[s] * used(8 * other + s, pair_total) for s in (2 * t, 2 * t + 1)], axis=0
        )
        w_high[8 + t], w_low[8 + t] = halves(w)

    def place_of(offset, rows):
        near_by = jnp.where(offset <= REACH, offset + REACH, offset - rows + REACH)
        return jnp.clip(jnp.where(offset == half, last, near_by), 0, last)

    dev_at, pair_at, partner_at = [], [], []
    for s in range(8):
        source = s_dev_list[0, s]
        offset = lax.rem(source // 2 - q + pairs, pairs)
        dev_at.append(2 * place_of(offset, pairs) + source % 2)
        pair_at.append(place_of(lax.rem(s_pair_list[0, s] - q + pairs, pairs), pairs))
        partner_at.append(place_of(lax.rem(partner_list[0, s] - q + pairs, pairs), pairs))

    everyone = tiles.at[pl.ds(0, count)]
    pltpu.make_async_copy(everyone, everyone, tile_recv).wait()
    root = jnp.zeros((16, 64), F32)

    def pair_tile(at):
        return tiles[2 * at] + tiles[2 * at + 1]

    for s in range(8):
        x = stacked(jnp.where(lane < 64, tiles[dev_at[s]], pair_tile(pair_at[s])))
        root += dot(x, w_high[s]) + dot(x, w_low[s])
    for t in range(4):
        low = pltpu.roll(pair_tile(partner_at[2 * t]), 64, 1)
        x = stacked(jnp.where(lane < 64, low, pair_tile(partner_at[2 * t + 1])))
        root += dot(x, w_high[8 + t]) + dot(x, w_low[8 + t])
    root = stacked(folded(root))
    far = folded(dot(root, down_high) + dot(root, down_low))
    for l in range(2):
        out[l] = near[l] + far[:, 256 * l : 256 * (l + 1)]

    pltpu.make_async_copy(everyone, everyone, tile_send).wait()
    for copy in others:
        copy.wait_send()


def per_device(*arrays):
    pairs = lax.axis_size("leaf")
    hbm = pl.BlockSpec(memory_space=pl.ANY)
    dma = pltpu.SemaphoreType.DMA
    return pl.pallas_call(
        functools.partial(kernel, pairs),
        out_shape=jax.ShapeDtypeStruct((2, 8, 256), F32),
        in_specs=[hbm] * len(arrays),
        out_specs=pl.BlockSpec(memory_space=pltpu.VMEM),
        scratch_shapes=[
            pltpu.VMEM((3, 2, 8, 256), BF16),
            pltpu.VMEM((2, 64, 256), BF16),
            pltpu.VMEM((1, 3, 64, 64), F32),
            pltpu.VMEM((2, 6, 256, 256), BF16),
            pltpu.VMEM((1, 8, 64, 64), F32),
            pltpu.VMEM((2, 1, 8, 64, 64), F32),
            pltpu.VMEM((24, 8, 128), F32),
            pltpu.VMEM((12, 128, 64), BF16),
            pltpu.VMEM((12, 128, 64), BF16),
            pltpu.SMEM((2, 6), jnp.int32),
            pltpu.SMEM((2,), jnp.int32),
            pltpu.SMEM((1, 8), jnp.int32),
            pltpu.SMEM((1,), jnp.int32),
            pltpu.SMEM((1, 8), jnp.int32),
            pltpu.SMEM((1,), jnp.int32),
            pltpu.SMEM((1, 8), jnp.int32),
            dma((13,)),
            dma,
            dma,
            dma((2,)),
            dma((2,)),
            dma,
            dma,
            dma,
            dma,
        ],
        compiler_params=pltpu.CompilerParams(
            collective_id=0, has_side_effects=True, vmem_limit_bytes=48 * 1024 * 1024
        ),
        name="h2_product",
    )(*arrays)


def solution(mesh):
    both = ("leaf", "grp")
    return jax.shard_map(
        per_device,
        mesh=mesh,
        in_specs=(
            P(both, None, None),
            P(both, None, None),
            P(both, None, None, None),
            P(both, None, None, None),
            P(both, None),
            P(both),
            P(both, None, None, None),
            P(both, None),
            P(both),
            P("leaf", "grp", None, None),
            P("leaf", "grp"),
            P("leaf"),
        ),
        out_specs=P(both, None, None),
        check_vma=False,
    )
```

time: 369 us -> 37.5 us (0.10)
  waiting for transfers between devices: 322 us -> 0 us
  Pallas kernels: 0 us -> 26.8 us
  starting transfers between devices: 16.5 us -> 0 us
  between operations: 14.8 us -> 1.32 us
  matrix products: 12.4 us -> 0 us
  local copies, waits for them, and re-layouts: 0.66 us -> 8.98 us
    all_gather x2 -> x0, waiting for transfers between devices: 321 us -> none  [the longest x1 163 us: per_device(): lax.all_gather(section_coeff, ('leaf', 'grp'), axis=0, tiled=True)]
    pallas_call x0 -> x1, Pallas kernels: none -> 26.8 us  [per_device(): pl.pallas_call(functools.partial(kernel, pairs), out_shape=jax.ShapeDtype...]
    ppermute x3 -> x0, starting transfers between devices: 16.5 us -> none  [the longest x1 12.4 us: extended_2(): after = lax.ppermute(first, axis, down)]
    dot_general x11 -> x0, matrix products: 12.4 us -> none  [the longest x1 3.29 us: per_device(): jnp.einsum('sn,nrk->srk', pick_pair, lift_piece, precision=exact_mode)]
    unnamed x14 -> x21, local copies, waits for them, and re-layouts: 0.03 us -> 8.98 us
  transfers between devices with their start and end apart: 5 -> 0, of which waited for: 2 -> 0; matrix products, arithmetic and copies ran while one was open for 3% -> 0% of each run, Pallas kernels for 0% -> 0%
where the time goes in v1:
time: 37.5 us; the launch traced here: 37.1 us
  Pallas kernels  26.8 us (71%)
  local copies, waits for them, and re-layouts  8.98 us (24%)
  between operations  1.32 us (4%)
    pallas_call x1, Pallas kernels, per_device(): pl.pallas_call(functools.partial(kernel, pairs), out_shape=jax.ShapeDtype...  26.8 us
    unnamed x21, local copies, waits for them, and re-layouts  8.98 us

profile of v1, /device:TPU:1, one launch (start us, length us, event | category | flops | bytes accessed | tf_op | source)
XLA Modules:
  0.0 37.1 jit_solution(5415337605198230414)
XLA Ops:
  1.3 0.0 copy-start
  1.3 1.4 %copy-done = bf16[2,6,256,256]{3,2,1,0:T(8,128)(2,1)S(1)} copy-done((bf16[2,6,256,256]{3,2,1,0:T(8,128)(2,1)S(1)}, bf16[2,6,256,256]{3,2,1,0:T(8,128)(2,1)}, u32[]{:S(2)}) %copy-start) | copy-done | bytes 1572888
  2.7 0.0 copy-start.1
  2.7 0.9 %copy-done.1 = f32[1,8,64,64]{3,2,1,0:T(8,128)S(1)} copy-done((f32[1,8,64,64]{3,2,1,0:T(8,128)S(1)}, f32[1,8,64,64]{3,2,1,0:T(8,128)}, u32[]{:S(2)}) %copy-start.1) | copy-done | bytes 131096
  3.7 0.0 copy-start.2
  3.7 0.9 %copy-done.2 = f32[1,8,64,64]{3,2,1,0:T(8,128)S(1)} copy-done((f32[1,8,64,64]{3,2,1,0:T(8,128)S(1)}, f32[1,8,64,64]{3,2,1,0:T(8,128)}, u32[]{:S(2)}) %copy-start.2) | copy-done | bytes 131096
  4.6 0.0 copy-start.3
  4.6 0.9 %copy-done.3 = f32[1,3,64,64]{3,2,1,0:T(8,128)S(1)} copy-done((f32[1,3,64,64]{3,2,1,0:T(8,128)S(1)}, f32[1,3,64,64]{3,2,1,0:T(8,128)}, u32[]{:S(2)}) %copy-start.3) | copy-done | bytes 49176
  5.5 0.0 copy-start.4
  5.5 0.8 %copy-done.4 = bf16[2,64,256]{2,1,0:T(8,128)(2,1)S(1)} copy-done((bf16[2,64,256]{2,1,0:T(8,128)(2,1)S(1)}, bf16[2,64,256]{2,1,0:T(8,128)(2,1)}, u32[]{:S(2)}) %copy-start.4) | copy-done | bytes 65560
  6.3 0.0 copy-start.5
  6.3 0.7 %copy-done.5 = bf16[2,8,256]{2,1,0:T(8,128)(2,1)S(1)} copy-done((bf16[2,8,256]{2,1,0:T(8,128)(2,1)S(1)}, bf16[2,8,256]{2,1,0:T(8,128)(2,1)}, u32[]{:S(2)}) %copy-start.5) | copy-done | bytes 8216
  7.0 0.0 copy-start.6
  7.0 0.7 %copy-done.6 = s32[2,6]{1,0:T(2,128)S(1)} copy-done((s32[2,6]{1,0:T(2,128)S(1)}, s32[2,6]{1,0:T(2,128)}, u32[]{:S(2)}) %copy-start.6) | copy-done | bytes 72
  7.7 0.0 copy-start.7
  7.7 0.7 %copy-done.7 = s32[2]{0:T(128)S(1)} copy-done((s32[2]{0:T(128)S(1)}, s32[2]{0:T(128)}, u32[]{:S(2)}) %copy-start.7) | copy-done | bytes 32
  8.4 0.0 copy-start.8
  8.4 0.7 %copy-done.8 = s32[1,8]{1,0:T(1,128)S(1)} copy-done((s32[1,8]{1,0:T(1,128)S(1)}, s32[1,8]{1,0:T(1,128)}, u32[]{:S(2)}) %copy-start.8) | copy-done | bytes 56
  9.0 0.0 copy-start.9
  9.0 0.7 %copy-done.9 = s32[1,8]{1,0:T(1,128)S(1)} copy-done((s32[1,8]{1,0:T(1,128)S(1)}, s32[1,8]{1,0:T(1,128)}, u32[]{:S(2)}) %copy-start.9) | copy-done | bytes 56
  9.7 26.8 %h2_product.1 = f32[2,8,256]{2,1,0:T(8,128)S(1)} custom-call(bf16[2,8,256]{2,1,0:T(8,128)(2,1)S(1)} %copy-done.5, bf16[2,64,256]{2,1,0:T(8,128)(2,1)S(1)} %copy-done.4, f32[1,3,64,64]{3,2,1,0:T(8,128)S(1)} %copy-done.3, bf16[2,6,256,256]{3,2,1,0:T(8,128)(2,1)S(1)} %copy-done, s32[2,6]{1,0:T(2,128)S(1)} %copy-done.6, s32[2]{0:T(128)S(1)} %copy-done.7, ...), custom_call_target="tpu_custom_call" | custom-call | tf_op jit(solution)/shard_map/h2_product/pallas_call | solution.py:281
  36.5 0.6 %copy.16 = f32[2,8,256]{2,1,0:T(8,128)} copy(f32[2,8,256]{2,1,0:T(8,128)S(1)} %h2_product.1) | data formatting | bytes 32768
Async XLA Ops:
  1.3 1.4 %copy-start = (bf16[2,6,256,256]{3,2,1,0:T(8,128)(2,1)S(1)}, bf16[2,6,256,256]{3,2,1,0:T(8,128)(2,1)}, u32[]{:S(2)}) copy-start(bf16[2,6,256,256]{3,2,1,0:T(8,128)(2,1)} %near_blocks.1) | copy-start | bytes 4718596
  2.7 0.9 %copy-start.1 = (f32[1,8,64,64]{3,2,1,0:T(8,128)S(1)}, f32[1,8,64,64]{3,2,1,0:T(8,128)}, u32[]{:S(2)}) copy-start(f32[1,8,64,64]{3,2,1,0:T(8,128)} %dev_coupling.1) | copy-start | bytes 393220
  3.7 0.9 %copy-start.2 = (f32[1,8,64,64]{3,2,1,0:T(8,128)S(1)}, f32[1,8,64,64]{3,2,1,0:T(8,128)}, u32[]{:S(2)}) copy-start(f32[1,8,64,64]{3,2,1,0:T(8,128)} %pair_coupling.1) | copy-start | bytes 393220
  4.6 0.9 %copy-start.3 = (f32[1,3,64,64]{3,2,1,0:T(8,128)S(1)}, f32[1,3,64,64]{3,2,1,0:T(8,128)}, u32[]{:S(2)}) copy-start(f32[1,3,64,64]{3,2,1,0:T(8,128)} %transfers.1) | copy-start | bytes 147460
  5.5 0.8 %copy-start.4 = (bf16[2,64,256]{2,1,0:T(8,128)(2,1)S(1)}, bf16[2,64,256]{2,1,0:T(8,128)(2,1)}, u32[]{:S(2)}) copy-start(bf16[2,64,256]{2,1,0:T(8,128)(2,1)} %basis.1) | copy-start | bytes 196612
  6.3 0.7 %copy-start.5 = (bf16[2,8,256]{2,1,0:T(8,128)(2,1)S(1)}, bf16[2,8,256]{2,1,0:T(8,128)(2,1)}, u32[]{:S(2)}) copy-start(bf16[2,8,256]{2,1,0:T(8,128)(2,1)} %charges.1) | copy-start | bytes 24580
  7.0 0.7 %copy-start.6 = (s32[2,6]{1,0:T(2,128)S(1)}, s32[2,6]{1,0:T(2,128)}, u32[]{:S(2)}) copy-start(s32[2,6]{1,0:T(2,128)} %near_list.1) | copy-start | bytes 148
  7.7 0.7 %copy-start.7 = (s32[2]{0:T(128)S(1)}, s32[2]{0:T(128)}, u32[]{:S(2)}) copy-start(s32[2]{0:T(128)} %near_count.1) | copy-start | bytes 28
  8.4 0.7 %copy-start.8 = (s32[1,8]{1,0:T(1,128)S(1)}, s32[1,8]{1,0:T(1,128)}, u32[]{:S(2)}) copy-start(s32[1,8]{1,0:T(1,128)} %dev_list.1) | copy-start | bytes 100
  9.0 0.7 %copy-start.9 = (s32[1,8]{1,0:T(1,128)S(1)}, s32[1,8]{1,0:T(1,128)}, u32[]{:S(2)}) copy-start(s32[1,8]{1,0:T(1,128)} %pair_list.1) | copy-start | bytes 100

commit v2 on v1

--- a/solution.py
+++ b/solution.py
@@ -62,8 +62,7 @@
     dev_buf,
     pair_buf,
     tiles,
-    w_high,
-    w_low,
+    weights,
     s_near_list,
     s_near_count,
     s_dev_list,
@@ -88,13 +87,28 @@
     own = REACH
     last = 2 * REACH + 1
 
-    peers = [((q, other), 2 * own + g)]
-    for shift in (half, 5, -5, 4, -4, 3, -3, 2, -2, 1, -1):
+    peers = [(q, other, 2 * own + g, True)]
+    side = 2 * g - 1
+    for shift, same, cross in (
+        (half, True, False),
+        (5, False, False),
+        (-5, False, False),
+        (4, False, False),
+        (-4, False, False),
+        (3 * side, False, True),
+        (-3 * side, False, False),
+        (2, True, True),
+        (-2, True, True),
+        (1, True, True),
+        (-1, True, True),
+    ):
         there = lax.rem(q + (shift + pairs), pairs)
-        place = last if shift == half else own - shift
-        for core in (g, other):
-            peers.append(((there, core), 2 * place + g))
+        place = 2 * (last if shift is half else own - shift) + g
+        peers.append((there, g, place, same))
+        peers.append((there, other, place, cross))
     count = len(peers)
+    whole_tiles = sum(whole for *_, whole in peers)
+    received = whole_tiles + (count - whole_tiles) // 2
 
     local = [
         (charges, charge_buf.at[1]),
@@ -115,8 +129,8 @@
     for copy in local[:3]:
         copy.start()
     barrier = pltpu.get_barrier_semaphore()
-    for device, _ in peers:
-        pl.semaphore_signal(barrier, inc=1, device_id=device, device_id_type=MESH)
+    for there, core, _, _ in peers:
+        pl.semaphore_signal(barrier, inc=1, device_id=(there, core), device_id_type=MESH)
     for copy in local[3:]:
         copy.start()
 
@@ -124,30 +138,38 @@
         copy.wait()
     e = transfer_buf[0]
     e01 = e[0:2].reshape(128, 64)
-    up = jnp.concatenate([e01, dot3(e01, e[2])], axis=1)
+    e012 = dot3(e01, e[2])
+    up_high, up_low = halves(jnp.concatenate([e012, e012, e01, e01], axis=1))
     own_charges = charge_buf[1].astype(F32).reshape(16, 256).astype(BF16)
-    cross = dot(own_charges, basis_buf[...].reshape(128, 256), NT)
+    products = dot(own_charges, basis_buf[...].reshape(128, 256), NT)
     lane = lax.broadcasted_iota(jnp.int32, (8, 128), 1)
-    leaf_coeff = stacked(jnp.where(lane < 64, cross[0:8], cross[8:16]))
-    up_high, up_low = halves(up)
+    row = lax.broadcasted_iota(jnp.int32, (8, 128), 0)
+    leaf_coeff = stacked(jnp.where(lane < 64, products[0:8], products[8:16]))
+    raised = folded(dot(leaf_coeff, up_high) + dot(leaf_coeff, up_low))
+    lift, coeff = raised[:, 0:128], raised[:, 128:256]
     my_tile = 2 * own + g
-    tiles[my_tile] = folded(dot(leaf_coeff, up_high) + dot(leaf_coeff, up_low))
+    straight = (row < 4) == (lane < 64)
+    tiles[my_tile] = jnp.where(
+        straight,
+        jnp.where(row < 4, lift, coeff),
+        pltpu.roll(jnp.where(row < 4, coeff, lift), 4, 0),
+    )
 
     pl.semaphore_wait(barrier, count)
     sends = []
-    for device, place in peers:
+    for there, core, place, whole in peers:
+        rows = pl.ds(0, 8 if whole else 4)
         sends.append(
             pltpu.make_async_remote_copy(
-                src_ref=tiles.at[my_tile],
-                dst_ref=tiles.at[place],
+                src_ref=tiles.at[my_tile, rows],
+                dst_ref=tiles.at[place, rows],
                 send_sem=tile_send,
                 recv_sem=tile_recv,
-                device_id=device,
+                device_id=(there, core),
                 device_id_type=MESH,
             )
         )
-    step = 2 * g - 1
-    beside = (lax.rem(q + step + pairs, pairs), other)
+    beside = (lax.rem(q + side + pairs, pairs), other)
     to_partner = pltpu.make_async_remote_copy(
         src_ref=charges,
         dst_ref=charge_buf.at[2 * g],
@@ -205,7 +227,7 @@
         w = jnp.concatenate(
             [dev_buf[0, s] * used(s, dev_total), lifted[s] * used(8 * g + s, pair_total)], axis=0
         )
-        w_high[s], w_low[s] = halves(w)
+        weights[s] = jnp.concatenate(halves(w), axis=1)
 
     down = [
         dot(e_part, basis_buf[l], TN)
@@ -213,7 +235,7 @@
         for e_part in halves(e[l])
     ]
     down = jnp.concatenate([down[0] + down[1], down[2] + down[3]], axis=1)
-    down_high, down_low = halves(down)
+    down = jnp.concatenate(halves(down), axis=0)
 
     for copy in (to_beside, to_partner):
         copy.wait_recv()
@@ -234,9 +256,9 @@
     lifted = through_pair(pair_buf[1, 0])
     for t in range(4):
         w = jnp.concatenate(
-            [lifted[s] * used(8 * other + s, pair_total) for s in (2 * t, 2 * t + 1)], axis=0
+            [lifted[s] * used(8 * other + s, pair_total) for s in (2 * t + 1, 2 * t)], axis=0
         )
-        w_high[8 + t], w_low[8 + t] = halves(w)
+        weights[8 + t] = jnp.concatenate(halves(w), axis=1)
 
     def place_of(offset, rows):
         near_by = jnp.where(offset <= REACH, offset + REACH, offset - rows + REACH)
@@ -250,22 +272,25 @@
         pair_at.append(place_of(lax.rem(s_pair_list[0, s] - q + pairs, pairs), pairs))
         partner_at.append(place_of(lax.rem(partner_list[0, s] - q + pairs, pairs), pairs))
 
-    everyone = tiles.at[pl.ds(0, count)]
+    everyone = tiles.at[pl.ds(0, received)]
     pltpu.make_async_copy(everyone, everyone, tile_recv).wait()
-    root = jnp.zeros((16, 64), F32)
 
     def pair_tile(at):
         return tiles[2 * at] + tiles[2 * at + 1]
 
+    def unpacked(tile):
+        return jnp.where(straight, pltpu.roll(tile, 4, 0), pltpu.roll(tile, 64, 1))
+
+    sources = []
     for s in range(8):
-        x = stacked(jnp.where(lane < 64, tiles[dev_at[s]], pair_tile(pair_at[s])))
-        root += dot(x, w_high[s]) + dot(x, w_low[s])
+        sources.append(unpacked(jnp.where(row < 4, pair_tile(pair_at[s]), tiles[dev_at[s]])))
     for t in range(4):
-        low = pltpu.roll(pair_tile(partner_at[2 * t]), 64, 1)
-        x = stacked(jnp.where(lane < 64, low, pair_tile(partner_at[2 * t + 1])))
-        root += dot(x, w_high[8 + t]) + dot(x, w_low[8 + t])
-    root = stacked(folded(root))
-    far = folded(dot(root, down_high) + dot(root, down_low))
+        first_pair, second_pair = pair_tile(partner_at[2 * t]), pair_tile(partner_at[2 * t + 1])
+        sources.append(unpacked(jnp.where(row < 4, first_pair, pltpu.roll(second_pair, 4, 0))))
+    sources = stacked(jnp.concatenate(sources, axis=1))
+    root = folded(dot(sources, weights[...].reshape(12 * 128, 128)))
+    root = stacked(root + pltpu.roll(root, 64, 1))
+    far = folded(dot(root, down))
     for l in range(2):
         out[l] = near[l] + far[:, 256 * l : 256 * (l + 1)]
 
@@ -291,8 +316,7 @@
             pltpu.VMEM((1, 8, 64, 64), F32),
             pltpu.VMEM((2, 1, 8, 64, 64), F32),
             pltpu.VMEM((24, 8, 128), F32),
-            pltpu.VMEM((12, 128, 64), BF16),
-            pltpu.VMEM((12, 128, 64), BF16),
+            pltpu.VMEM((12, 128, 128), BF16),
             pltpu.SMEM((2, 6), jnp.int32),
             pltpu.SMEM((2,), jnp.int32),
             pltpu.SMEM((1, 8), jnp.int32),
@@ -311,10 +335,10 @@
             dma,
         ],
         compiler_params=pltpu.CompilerParams(
-            collective_id=0, has_side_effects=True, vmem_limit_bytes=48 * 1024 * 1024
+            collective_id=0, has_side_effects=True, vmem_limit_bytes=32 * 1024 * 1024
         ),
         name="h2_product",
-    )(*arrays)
+    )(*[a if a.size == 1 else pltpu.with_memory_space_constraint(a, pltpu.HBM) for a in arrays])
 
 
 def solution(mesh):

time: 37.5 us -> 28.3 us (0.75)
  local copies, waits for them, and re-layouts: 8.98 us -> 0.61 us
  Pallas kernels: 26.8 us -> 26.2 us
    unnamed x21 -> x1, local copies, waits for them, and re-layouts: 8.98 us -> 0.61 us
    pallas_call x1, Pallas kernels: 26.8 us -> 26.2 us  [per_device(): pl.pallas_call(functools.partial(kernel, pairs), out_shape=jax.ShapeDtype...]
where the time goes in v2:
time: 28.3 us; the launch traced here: 28.1 us
  Pallas kernels  26.2 us (93%)
  between operations  1.3 us (5%)
  local copies, waits for them, and re-layouts  0.61 us (2%)
    pallas_call x1, Pallas kernels, per_device(): pl.pallas_call(functools.partial(kernel, pairs), out_shape=jax.ShapeDtype...  26.2 us
    unnamed x1, local copies, waits for them, and re-layouts  0.61 us

profile of v2, /device:TPU:1, one launch (start us, length us, event | category | flops | bytes accessed | tf_op | source)
XLA Modules:
  0.0 28.1 jit_solution(4914747777250181489)
XLA Ops:
  1.3 26.2 %h2_product.1 = f32[2,8,256]{2,1,0:T(8,128)S(1)} custom-call(bf16[2,8,256]{2,1,0:T(8,128)(2,1)} %charges.1, bf16[2,64,256]{2,1,0:T(8,128)(2,1)} %basis.1, f32[1,3,64,64]{3,2,1,0:T(8,128)} %transfers.1, bf16[2,6,256,256]{3,2,1,0:T(8,128)(2,1)} %near_blocks.1, s32[2,6]{1,0:T(2,128)} %near_list.1, s32[2]{0:T(128)} %near_count.1, f32[1,8,64,64]{3,2,1,0:T(8,128)} %dev_coupling.1, ...), custom_call_target="tpu_custom_call" | custom-call | tf_op jit(solution)/shard_map/h2_product/pallas_call | solution.py:306
  27.5 0.6 %copy.16 = f32[2,8,256]{2,1,0:T(8,128)} copy(f32[2,8,256]{2,1,0:T(8,128)S(1)} %h2_product.1) | data formatting | bytes 32768

commit v3 on v2

--- a/solution.py
+++ b/solution.py
@@ -38,6 +38,11 @@
 
 def folded(a):
     return a[0:8] + a[8:16]
+
+
+def wrapped(at, rows):
+    at = jnp.where(at < 0, at + rows, at)
+    return jnp.where(at < rows, at, at - rows)
 
 
 def kernel(
@@ -62,7 +67,8 @@
     dev_buf,
     pair_buf,
     tiles,
-    weights,
+    dev_weights,
+    pair_weights,
     s_near_list,
     s_near_count,
     s_dev_list,
@@ -87,25 +93,26 @@
     own = REACH
     last = 2 * REACH + 1
 
-    peers = [(q, other, 2 * own + g, True)]
     side = 2 * g - 1
+    peers = []
     for shift, same, cross in (
-        (half, True, False),
-        (5, False, False),
-        (-5, False, False),
-        (4, False, False),
-        (-4, False, False),
+        (2, True, True),
+        (1, True, True),
         (3 * side, False, True),
         (-3 * side, False, False),
-        (2, True, True),
+        (4, False, False),
+        (5, False, False),
+        (half, True, False),
+        (-1, True, True),
         (-2, True, True),
-        (1, True, True),
-        (-1, True, True),
+        (-4, False, False),
+        (-5, False, False),
     ):
-        there = lax.rem(q + (shift + pairs), pairs)
+        there = wrapped(q + shift, pairs)
         place = 2 * (last if shift is half else own - shift) + g
         peers.append((there, g, place, same))
         peers.append((there, other, place, cross))
+    peers.append((q, other, 2 * own + g, True))
     count = len(peers)
     whole_tiles = sum(whole for *_, whole in peers)
     received = whole_tiles + (count - whole_tiles) // 2
@@ -169,7 +176,7 @@
                 device_id_type=MESH,
             )
         )
-    beside = (lax.rem(q + side + pairs, pairs), other)
+    beside = (wrapped(q + side, pairs), other)
     to_partner = pltpu.make_async_remote_copy(
         src_ref=charges,
         dst_ref=charge_buf.at[2 * g],
@@ -203,74 +210,63 @@
         device_id_type=MESH,
     )
     others = [to_beside, to_partner, give_coupling, give_list]
-    for copy in sends + others:
+    for copy in others[:2] + sends[:8] + others[2:] + sends[8:]:
         copy.start()
 
     for copy in local[3:5]:
         copy.wait()
     for copy in local[7:]:
         copy.wait()
-    e2h, e2l = halves(e[2])
-
-    def through_pair(blocks):
-        rows = blocks.reshape(512, 64)
-        rh, rl = halves(rows)
-        return (dot(rh, e2h, NT) + dot(rl, e2h, NT) + dot(rh, e2l, NT)).reshape(8, 64, 64)
 
     def used(slot, total):
         return jnp.where(slot < total, 1.0, 0.0).astype(F32)
 
+    def weigh(coupling, slot, total):
+        return jnp.concatenate(halves(coupling * used(slot, total)), axis=1)
+
     dev_total = s_dev_count[0]
     pair_total = s_pair_count[0]
-    lifted = through_pair(pair_buf[0, 0])
     for s in range(8):
-        w = jnp.concatenate(
-            [dev_buf[0, s] * used(s, dev_total), lifted[s] * used(8 * g + s, pair_total)], axis=0
-        )
-        weights[s] = jnp.concatenate(halves(w), axis=1)
-
-    down = [
-        dot(e_part, basis_buf[l], TN)
-        for l in range(2)
-        for e_part in halves(e[l])
-    ]
-    down = jnp.concatenate([down[0] + down[1], down[2] + down[3]], axis=1)
+        dev_weights[s] = weigh(dev_buf[0, s], s, dev_total)
+        pair_weights[s] = weigh(pair_buf[0, 0, s], 8 * g + s, pair_total)
+
+    down = []
+    for l in range(2):
+        high, low = halves(e[l])
+        down.append(dot(high, basis_buf[l], TN) + dot(low, basis_buf[l], TN))
+    down = jnp.concatenate(down, axis=1)
+    down = jnp.concatenate([down, dot3(e[2], down, TN)], axis=0)
     down = jnp.concatenate(halves(down), axis=0)
 
     for copy in (to_beside, to_partner):
         copy.wait_recv()
     for copy in local[5:7]:
         copy.wait()
-    first = 2 * (2 * q + g) - 2
+    lowest = 2 * (2 * q + g) - 2
     near = []
     for l in range(2):
         total = jnp.zeros((8, 256), F32)
         for s in range(6):
-            at = jnp.clip(s_near_list[l, s] - first, 0, 5)
+            at = jnp.clip(s_near_list[l, s] - lowest, 0, 5)
             picked = charge_buf[at // 2, at % 2].astype(F32) * used(s, s_near_count[l])
             total += dot(picked.astype(BF16), block_buf[l, s])
         near.append(total)
 
     give_coupling.wait_recv()
     give_list.wait_recv()
-    lifted = through_pair(pair_buf[1, 0])
-    for t in range(4):
-        w = jnp.concatenate(
-            [lifted[s] * used(8 * other + s, pair_total) for s in (2 * t + 1, 2 * t)], axis=0
-        )
-        weights[8 + t] = jnp.concatenate(halves(w), axis=1)
-
-    def place_of(offset, rows):
-        near_by = jnp.where(offset <= REACH, offset + REACH, offset - rows + REACH)
-        return jnp.clip(jnp.where(offset == half, last, near_by), 0, last)
-
-    dev_at, pair_at, partner_at = [], [], []
+    for s in range(8):
+        pair_weights[8 + s] = weigh(pair_buf[1, 0, s], 8 * other + s, pair_total)
+
+    def place_of(source):
+        offset = source - q
+        offset = jnp.where(offset > half, offset - pairs, jnp.where(offset < -half, offset + pairs, offset))
+        return jnp.clip(jnp.where(jnp.abs(offset) == half, last, offset + own), 0, last)
+
+    dev_at = []
     for s in range(8):
         source = s_dev_list[0, s]
-        offset = lax.rem(source // 2 - q + pairs, pairs)
-        dev_at.append(2 * place_of(offset, pairs) + source % 2)
-        pair_at.append(place_of(lax.rem(s_pair_list[0, s] - q + pairs, pairs), pairs))
-        partner_at.append(place_of(lax.rem(partner_list[0, s] - q + pairs, pairs), pairs))
+        dev_at.append(2 * place_of(source >> 1) + (source & 1))
+    pair_at = [place_of(ref[0, s]) for ref in (s_pair_list, partner_list) for s in range(8)]
 
     everyone = tiles.at[pl.ds(0, received)]
     pltpu.make_async_copy(everyone, everyone, tile_recv).wait()
@@ -281,16 +277,24 @@
     def unpacked(tile):
         return jnp.where(straight, pltpu.roll(tile, 4, 0), pltpu.roll(tile, 64, 1))
 
-    sources = []
-    for s in range(8):
-        sources.append(unpacked(jnp.where(row < 4, pair_tile(pair_at[s]), tiles[dev_at[s]])))
-    for t in range(4):
-        first_pair, second_pair = pair_tile(partner_at[2 * t]), pair_tile(partner_at[2 * t + 1])
-        sources.append(unpacked(jnp.where(row < 4, first_pair, pltpu.roll(second_pair, 4, 0))))
-    sources = stacked(jnp.concatenate(sources, axis=1))
-    root = folded(dot(sources, weights[...].reshape(12 * 128, 128)))
-    root = stacked(root + pltpu.roll(root, 64, 1))
-    far = folded(dot(root, down))
+    dev_sources, pair_sources = [], []
+    for t in range(0, 8, 2):
+        first, second = (tiles[dev_at[s]] for s in (t, t + 1))
+        dev_sources.append(unpacked(jnp.where(row < 4, pltpu.roll(second, 4, 0), first)))
+    for t in range(0, 16, 2):
+        first, second = (pair_tile(pair_at[s]) for s in (t, t + 1))
+        pair_sources.append(unpacked(jnp.where(row < 4, second, pltpu.roll(first, 4, 0))))
+
+    def gathered(sources, weights, slots):
+        sources = stacked(jnp.concatenate(sources, axis=1))
+        sums = folded(dot(sources, weights[...].reshape(slots * 64, 128)))
+        return sums + pltpu.roll(sums, 64, 1)
+
+    field = jnp.where(
+        lane < 64, gathered(dev_sources, dev_weights, 8), gathered(pair_sources, pair_weights, 16)
+    )
+    field = stacked(field)
+    far = folded(dot(jnp.concatenate([field, field], axis=1), down))
     for l in range(2):
         out[l] = near[l] + far[:, 256 * l : 256 * (l + 1)]
 
@@ -316,7 +320,8 @@
             pltpu.VMEM((1, 8, 64, 64), F32),
             pltpu.VMEM((2, 1, 8, 64, 64), F32),
             pltpu.VMEM((24, 8, 128), F32),
-            pltpu.VMEM((12, 128, 128), BF16),
+            pltpu.VMEM((8, 64, 128), BF16),
+            pltpu.VMEM((16, 64, 128), BF16),
             pltpu.SMEM((2, 6), jnp.int32),
             pltpu.SMEM((2,), jnp.int32),
             pltpu.SMEM((1, 8), jnp.int32),

time: 28.3 us -> 27.8 us (0.982)
  Pallas kernels: 26.2 us -> 25.7 us
    pallas_call x1, Pallas kernels: 26.2 us -> 25.7 us  [per_device(): pl.pallas_call(functools.partial(kernel, pairs), out_shape=jax.ShapeDtype...]
where the time goes in v3:
time: 27.8 us; the launch traced here: 27.6 us
  Pallas kernels  25.7 us (92%)
  between operations  1.3 us (5%)
  local copies, waits for them, and re-layouts  0.61 us (2%)
    pallas_call x1, Pallas kernels, per_device(): pl.pallas_call(functools.partial(kernel, pairs), out_shape=jax.ShapeDtype...  25.7 us
    unnamed x1, local copies, waits for them, and re-layouts  0.61 us

profile of v3, /device:TPU:1, one launch (start us, length us, event | category | flops | bytes accessed | tf_op | source)
XLA Modules:
  0.0 27.6 jit_solution(16900186397815469233)
XLA Ops:
  1.3 25.7 %h2_product.1 = f32[2,8,256]{2,1,0:T(8,128)S(1)} custom-call(bf16[2,8,256]{2,1,0:T(8,128)(2,1)} %charges.1, bf16[2,64,256]{2,1,0:T(8,128)(2,1)} %basis.1, f32[1,3,64,64]{3,2,1,0:T(8,128)} %transfers.1, bf16[2,6,256,256]{3,2,1,0:T(8,128)(2,1)} %near_blocks.1, s32[2,6]{1,0:T(2,128)} %near_list.1, s32[2]{0:T(128)} %near_count.1, f32[1,8,64,64]{3,2,1,0:T(8,128)} %dev_coupling.1, ...), custom_call_target="tpu_custom_call" | custom-call | tf_op jit(solution)/shard_map/h2_product/pallas_call | solution.py:310
  27.0 0.6 %copy.16 = f32[2,8,256]{2,1,0:T(8,128)} copy(f32[2,8,256]{2,1,0:T(8,128)S(1)} %h2_product.1) | data formatting | bytes 32768
